TPU v7x, 256 devices: a whole 4x4x8 slice. The times are simulated.
256 devices in a mesh: ctx: 32 (over x, z), head: 8 (over y, core).
Axes of the slice: x: 4, y: 4, z: 8, core: 2. Of those that a mesh axis runs over, the one named last changes fastest.
Arguments:
- queries: bfloat16 [32768, 4096], P(('ctx', 'head')), may hold values from -6 to 6
- key_rows: bfloat16 [32768, 4096], P(('ctx', 'head')), may hold values from -6 to 6
- value_rows: bfloat16 [32768, 4096], P(('ctx', 'head')), may hold values from -6 to 6
- out_grad: bfloat16 [32768, 4096], P(('ctx', 'head')), may hold values from -6 to 6
Outputs:
- attended: bfloat16 [32768, 4096], P('ctx', 'head')
- query_grad: bfloat16 [32768, 4096], P('ctx', 'head')
- key_grad: bfloat16 [32768, 4096], P('ctx', 'head')
- value_grad: bfloat16 [32768, 4096], P('ctx', 'head')
All inputs are finite; a program needn't handle non-finite values.
Results may differ from a plain program's by a relative error of at most 0.0049.
Values may be sent and summed in bfloat16 or wider, within the bound.
A program may use at most 128 MiB of HBM per device.

v0:
```python
import math

import jax
import jax.numpy as jnp
from jax import lax
from jax.sharding import PartitionSpec as P

HD = 128


def entering(part, axis, combine, identity, reverse):
    count = lax.axis_size(axis)
    place = lax.axis_index(axis)
    ahead = count - 1 - place if reverse else place
    gathered = lax.all_gather(part, axis)
    state = jnp.zeros_like(part) + jnp.asarray(identity, part.dtype)

    def one(lap, state):
        source = count - 1 - lap if reverse else lap
        return combine(state, lax.dynamic_index_in_dim(gathered, source, 0, False))

    return lax.fori_loop(0, ahead, one, state)


def add_states(earlier, later):
    return earlier + later


def contract(left, right, left_dim, right_dim):
    return lax.dot_general(
        left, right, (((left_dim,), (right_dim,)), ((), ())), preferred_element_type=jnp.float32
    )


def on_device(queries, key_rows, value_rows, out_grad):
    query_loc, key_loc, value_loc, grad_loc = (
        lax.all_to_all(queries, "head", split_axis=1, concat_axis=0, tiled=True),
        lax.all_to_all(key_rows, "head", split_axis=1, concat_axis=0, tiled=True),
        lax.all_to_all(value_rows, "head", split_axis=1, concat_axis=0, tiled=True),
        lax.all_to_all(out_grad, "head", split_axis=1, concat_axis=0, tiled=True),
    )
    count = query_loc.shape[0]
    group = query_loc.shape[1] // HD
    scale = 1.0 / math.sqrt(HD * count * lax.axis_size("ctx"))
    kv_state = jnp.einsum(
        "thd,the->hde",
        key_loc.reshape(count, group, HD),
        value_loc.reshape(count, group, HD),
        preferred_element_type=jnp.float32,
    )
    qg_state = jnp.einsum(
        "thd,the->hde",
        query_loc.reshape(count, group, HD),
        grad_loc.reshape(count, group, HD),
        preferred_element_type=jnp.float32,
    )
    zeros_state = jnp.zeros_like(kv_state)
    prefix = entering(kv_state, "ctx", add_states, zeros_state, False)
    suffix = entering(qg_state, "ctx", add_states, zeros_state, True)
    prefix_b = (scale * prefix).astype(jnp.bfloat16)
    suffix_b = (scale * suffix).astype(jnp.bfloat16)
    causal = lax.broadcasted_iota(jnp.int32, (count, count), 0) >= lax.broadcasted_iota(
        jnp.int32, (count, count), 1
    )
    outputs, dqueries, dkeys, dvalues = ([], [], [], [])
    for head_index in range(group):
        lower = head_index * HD
        query_h = query_loc[:, lower : lower + HD]
        key_h = key_loc[:, lower : lower + HD]
        value_h = value_loc[:, lower : lower + HD]
        grad_h = grad_loc[:, lower : lower + HD]
        prefix_h = prefix_b[head_index]
        suffix_h = suffix_b[head_index]
        attn_b = jnp.where(causal, contract(query_h, key_h, 1, 1) * scale, 0.0).astype(jnp.bfloat16)
        back_b = jnp.where(causal, contract(grad_h, value_h, 1, 1) * scale, 0.0).astype(
            jnp.bfloat16
        )
        outputs.append(
            (
                jnp.dot(attn_b, value_h, preferred_element_type=jnp.float32)
                + jnp.dot(query_h, prefix_h, preferred_element_type=jnp.float32)
            ).astype(jnp.bfloat16)
        )
        dqueries.append(
            (
                jnp.dot(back_b, key_h, preferred_element_type=jnp.float32)
                + contract(grad_h, prefix_h, 1, 1)
            ).astype(jnp.bfloat16)
        )
        dkeys.append(
            (contract(back_b, query_h, 0, 0) + contract(value_h, suffix_h, 1, 1)).astype(
                jnp.bfloat16
            )
        )
        dvalues.append(
            (
                contract(attn_b, grad_h, 0, 0)
                + jnp.dot(key_h, suffix_h, preferred_element_type=jnp.float32)
            ).astype(jnp.bfloat16)
        )
    return (
        jnp.concatenate(outputs, axis=1),
        jnp.concatenate(dqueries, axis=1),
        jnp.concatenate(dkeys, axis=1),
        jnp.concatenate(dvalues, axis=1),
    )


def solution(mesh):
    placed = (
        P(("ctx", "head"), None),
        P(("ctx", "head"), None),
        P(("ctx", "head"), None),
        P(("ctx", "head"), None),
    )
    return jax.shard_map(
        on_device,
        mesh=mesh,
        in_specs=placed,
        out_specs=(P("ctx", "head"), P("ctx", "head"), P("ctx", "head"), P("ctx", "head")),
        check_vma=False,
    )
```

profile of v0, /device:TPU:1, one launch (start us, length us, event | category | flops | bytes accessed | tf_op | source)
XLA Modules:
  0.0 310.6 jit_solution(14006105559594961525)
XLA Ops:
  7.2 2.4 copy.56
  9.5 6.7 %all-to-all-start.1 = ((bf16[128,8,512]{0,2,1:T(8,128)(2,1)}), bf16[128,8,512]{0,2,1:T(8,128)(2,1)S(1)}, u32[]{:S(2)}, u32[]{:S(2)}) async-start(bf16[128,8,512]{0,2,1:T(8,128)(2,1)} %bitcast.5), calls=%async_computation.1 | async-start | bytes 2097152 | tf_op jit(solution)/shard_map/all_to_all | solution.py:38
  16.2 1.3 copy.58
  17.5 13.8 %all-to-all-done.1 = bf16[128,8,512]{0,2,1:T(8,128)(2,1)S(1)} async-done(((bf16[128,8,512]{0,2,1:T(8,128)(2,1)}), bf16[128,8,512]{0,2,1:T(8,128)(2,1)S(1)}, u32[]{:S(2)}, u32[]{:S(2)}) %all-to-all-start.1) | async-done | bytes 1048608 | tf_op jit(solution)/shard_map/all_to_all | solution.py:38
  31.3 4.3 %all-to-all-start.2 = ((bf16[128,8,512]{0,2,1:T(8,128)(2,1)}), bf16[128,8,512]{0,2,1:T(8,128)(2,1)S(1)}, u32[]{:S(2)}, u32[]{:S(2)}) async-start(bf16[128,8,512]{0,2,1:T(8,128)(2,1)} %bitcast.8), calls=%async_computation.2 | async-start | bytes 2097152 | tf_op jit(solution)/shard_map/all_to_all | solution.py:39
  35.7 1.6 copy.60
  37.3 1.5 reshape.36
  38.9 11.9 %all-to-all-done.2 = bf16[128,8,512]{0,2,1:T(8,128)(2,1)S(1)} async-done(((bf16[128,8,512]{0,2,1:T(8,128)(2,1)}), bf16[128,8,512]{0,2,1:T(8,128)(2,1)S(1)}, u32[]{:S(2)}, u32[]{:S(2)}) %all-to-all-start.2) | async-done | bytes 1048608 | tf_op jit(solution)/shard_map/all_to_all | solution.py:39
  50.8 1.6 copy.61
  52.4 2.3 reshape.37
  54.7 2.4 fusion.96
  57.1 2.3 copy.54
  59.4 4.3 %all-to-all-start = ((bf16[128,8,512]{0,2,1:T(8,128)(2,1)}), bf16[128,8,512]{0,2,1:T(8,128)(2,1)S(1)}, u32[]{:S(2)}, u32[]{:S(2)}) async-start(bf16[128,8,512]{0,2,1:T(8,128)(2,1)} %bitcast.235), calls=%async_computation | async-start | bytes 2097152 | tf_op jit(solution)/shard_map/all_to_all | solution.py:37
  63.7 2.3 copy.63
  66.0 12.9 %all-to-all-done = bf16[128,8,512]{0,2,1:T(8,128)(2,1)S(1)} async-done(((bf16[128,8,512]{0,2,1:T(8,128)(2,1)}), bf16[128,8,512]{0,2,1:T(8,128)(2,1)S(1)}, u32[]{:S(2)}, u32[]{:S(2)}) %all-to-all-start) | async-done | bytes 1048608 | tf_op jit(solution)/shard_map/all_to_all | solution.py:37
  78.8 5.0 %all-to-all-start.3 = ((bf16[128,8,512]{0,2,1:T(8,128)(2,1)}), bf16[128,8,512]{0,2,1:T(8,128)(2,1)}, u32[]{:S(2)}, u32[]{:S(2)}) async-start(bf16[128,8,512]{0,2,1:T(8,128)(2,1)} %bitcast.234), calls=%async_computation.3 | async-start | bytes 2097152 | tf_op jit(solution)/shard_map/all_to_all | solution.py:40
  83.8 1.6 copy.65
  85.5 2.3 reshape.38
  87.8 11.3 %all-to-all-done.3 = bf16[128,8,512]{0,2,1:T(8,128)(2,1)} async-done(((bf16[128,8,512]{0,2,1:T(8,128)(2,1)}), bf16[128,8,512]{0,2,1:T(8,128)(2,1)}, u32[]{:S(2)}, u32[]{:S(2)}) %all-to-all-start.3) | async-done | bytes 1048608 | tf_op jit(solution)/shard_map/all_to_all | solution.py:40
  99.1 3.0 copy.66
  102.0 2.3 reshape.39
  104.3 2.4 fusion.97
  106.7 1.3 copy.59
  108.0 1.7 copy.64
  109.7 1.5 copy.55
  111.2 1.3 copy.57
  112.5 1.8 select_convert_fusion
  120.1 1.3 fusion.56
  121.4 1.6 fusion.53
  123.0 1.3 fusion.68
  124.3 1.6 fusion.65
  126.0 1.3 fusion.80
  127.3 1.6 fusion.77
  128.9 1.3 fusion.92
  130.2 1.6 fusion.89
  131.9 1.3 fusion.32
  133.2 1.6 fusion.50
  134.8 1.3 fusion.36
  136.1 1.7 fusion.62
  137.8 1.3 fusion.40
  139.1 1.6 fusion.74
  140.7 1.5 fusion.44
  142.2 1.6 fusion.86
  143.9 11.7 %all-gather.5.cloned.1.call-done = f32[128,128,128]{2,1,0:T(8,128)} async-done(((f32[4,128,128]{2,1,0:T(8,128)}), f32[128,128,128]{2,1,0:T(8,128)}) %all-gather.5.cloned.1.call-update) | async-done | bytes 8388624 | tf_op jit(solution)/shard_map/all_gather | solution.py:15
  155.6 97.9 %all-gather.7.cloned.1.call-done = f32[128,128,128]{2,1,0:T(8,128)} async-done(((f32[4,128,128]{2,1,0:T(8,128)}), f32[128,128,128]{2,1,0:T(8,128)}) %all-gather.7.cloned.1.call-update) | async-done | bytes 8388624 | tf_op jit(solution)/shard_map/all_gather | solution.py:15
  253.5 32.0 %while.23 = (s32[]{:T(128)}, f32[4,128,128]{2,1,0:T(8,128)S(1)}, s32[]{:T(128)}, f32[32,4,128,128]{3,2,1,0:T(8,128)}, s32[]{:T(128)}, /*index=5*/s32[]{:T(128)}, s32[]{:T(128)}, s32[]{:T(128)}) while((s32[]{:T(128)}, f32[4,128,128]{2,1,0:T(8,128)S(1)}, s32[]{:T(128)}, f32[32,4,128,128]{3,2,1,0:T(8,128)}, s32[]{:T(128)}, /*index=5*/s32[]{:T(128)}, ...), condition=%wide.region_3.4_spmd, body=%wide.region_2.3_spmd.sunk | while | flops 65542 | bytes 786575 | solution.py:22
  253.6 1.0 bitcast_add_fusion.5
  254.6 1.0 bitcast_add_fusion.5
  261.8 1.0 bitcast_add_fusion.5
  262.9 1.0 bitcast_add_fusion.5
  263.9 1.0 bitcast_add_fusion.5
  272.2 1.0 bitcast_add_fusion.5
  273.2 1.0 bitcast_add_fusion.5
  274.2 1.0 bitcast_add_fusion.5
  281.5 1.0 bitcast_add_fusion.5
  285.6 1.4 fusion.23
  287.0 2.0 fusion.22
  292.0 1.3 copy.70
  293.4 1.2 pad_maximum_fusion.1
  294.6 1.3 copy.69
  295.9 1.4 fusion.19
  297.3 1.3 fusion.31
  301.1 1.3 copy.71
  302.5 1.3 copy.68
  (95 shorter events, 33.4 us)
Async XLA Ops:
  7.2 9.1 %copy-start.19 = (bf16[128,4096]{1,0:T(8,128)(2,1)S(1)}, bf16[128,4096]{1,0:T(8,128)(2,1)}, u32[]{:S(2)}) copy-start(bf16[128,4096]{1,0:T(8,128)(2,1)} %param.10) | copy-start | bytes 3145732
  9.5 21.8 %all-to-all-start.1 = ((bf16[128,8,512]{0,2,1:T(8,128)(2,1)}), bf16[128,8,512]{0,2,1:T(8,128)(2,1)S(1)}, u32[]{:S(2)}, u32[]{:S(2)}) async-start(bf16[128,8,512]{0,2,1:T(8,128)(2,1)} %bitcast.5), calls=%async_computation.1 | async-start | bytes 2097152 | tf_op jit(solution)/shard_map/all_to_all | solution.py:38
  31.3 19.5 %all-to-all-start.2 = ((bf16[128,8,512]{0,2,1:T(8,128)(2,1)}), bf16[128,8,512]{0,2,1:T(8,128)(2,1)S(1)}, u32[]{:S(2)}, u32[]{:S(2)}) async-start(bf16[128,8,512]{0,2,1:T(8,128)(2,1)} %bitcast.8), calls=%async_computation.2 | async-start | bytes 2097152 | tf_op jit(solution)/shard_map/all_to_all | solution.py:39
  35.7 119.8 %all-gather.5.cloned.1.call-start = ((), (), s32[]{:S(2)}) async-start(), calls=%async_computation.4 | async-start | bytes 8650752 | tf_op jit(solution)/shard_map/all_gather | solution.py:15
  59.4 19.5 %all-to-all-start = ((bf16[128,8,512]{0,2,1:T(8,128)(2,1)}), bf16[128,8,512]{0,2,1:T(8,128)(2,1)S(1)}, u32[]{:S(2)}, u32[]{:S(2)}) async-start(bf16[128,8,512]{0,2,1:T(8,128)(2,1)} %bitcast.235), calls=%async_computation | async-start | bytes 2097152 | tf_op jit(solution)/shard_map/all_to_all | solution.py:37
  78.8 6.7 %copy-start = (bf16[128,8,512]{0,2,1:T(8,128)(2,1)}, bf16[128,8,512]{0,2,1:T(8,128)(2,1)S(1)}, u32[]{:S(2)}) copy-start(bf16[128,8,512]{0,2,1:T(8,128)(2,1)S(1)} %all-to-all-done) | copy-start | bytes 3145732
  78.8 20.2 %all-to-all-start.3 = ((bf16[128,8,512]{0,2,1:T(8,128)(2,1)}), bf16[128,8,512]{0,2,1:T(8,128)(2,1)}, u32[]{:S(2)}, u32[]{:S(2)}) async-start(bf16[128,8,512]{0,2,1:T(8,128)(2,1)} %bitcast.234), calls=%async_computation.3 | async-start | bytes 2097152 | tf_op jit(solution)/shard_map/all_to_all | solution.py:40
  83.8 169.7 %all-gather.7.cloned.1.call-start = ((), (), s32[]{:S(2)}) async-start(), calls=%async_computation.5 | async-start | bytes 8650752 | tf_op jit(solution)/shard_map/all_gather | solution.py:15
  99.1 5.3 %copy-start.4 = (bf16[1024,4,128]{0,2,1:T(8,128)(2,1)S(1)}, bf16[1024,4,128]{0,2,1:T(8,128)(2,1)}, u32[]{:S(2)}) copy-start(bf16[1024,4,128]{0,2,1:T(8,128)(2,1)} %reshape.38) | copy-start | bytes 3145732
  112.5 1.8 copy-start.1
  115.8 1.2 copy-start.2
  285.6 3.5 %copy-start.9 = (f32[1024,128]{0,1:T(8,128)S(1)}, f32[1024,128]{0,1:T(8,128)}, u32[]{:S(2)}) copy-start(f32[1024,128]{0,1:T(8,128)} %fusion.56) | copy-start | bytes 1572868
  285.6 3.7 %copy-start.11 = (f32[1024,128]{0,1:T(8,128)S(1)}, f32[1024,128]{0,1:T(8,128)}, u32[]{:S(2)}) copy-start(f32[1024,128]{0,1:T(8,128)} %fusion.68) | copy-start | bytes 1572868
  285.6 6.1 %copy-start.17 = (bf16[4,128,128]{2,1,0:T(8,128)(2,1)}, bf16[4,128,128]{2,1,0:T(8,128)(2,1)S(1)}, u32[]{:S(2)}) copy-start(bf16[4,128,128]{2,1,0:T(8,128)(2,1)S(1)} %multiply_convert_fusion) | copy-start | bytes 393220
  285.6 3.9 %copy-start.16 = (f32[1024,128]{0,1:T(8,128)S(1)}, f32[1024,128]{0,1:T(8,128)}, u32[]{:S(2)}) copy-start(f32[1024,128]{0,1:T(8,128)} %fusion.77) | copy-start | bytes 1572868
  287.0 3.5 %copy-start.10 = (f32[1024,128]{0,1:T(8,128)S(1)}, f32[1024,128]{0,1:T(8,128)}, u32[]{:S(2)}) copy-start(f32[1024,128]{0,1:T(8,128)} %fusion.80) | copy-start | bytes 1572868
  289.1 1.7 copy-start.15
  289.3 2.4 copy-start.8
  294.5 2.8 copy-start.3
  294.6 2.8 copy-start.18
  295.9 2.8 copy-start.14
  295.9 3.1 copy-start.7
  295.9 3.3 %copy-start.13 = (f32[1024,128]{0,1:T(8,128)S(1)}, f32[1024,128]{0,1:T(8,128)}, u32[]{:S(2)}) copy-start(f32[1024,128]{0,1:T(8,128)} %fusion.74) | copy-start | bytes 1572868
  297.3 2.2 copy-start.6
  298.7 1.1 copy-start.12
  299.0 1.7 copy-start.5
  301.0 1.4 copy-start.20
Sparse Core Ops, SparseCore 0:
  57.2 98.2 all-gather.4
  158.1 95.3 all-gather.6
where the time goes:
time: 312 us; the launch traced here: 311 us
  waiting for transfers between devices  160 us (51%)
  matrix products  46.6 us (15%)
  local copies, waits for them, and re-layouts  36.1 us (12%)
  other arithmetic  32.8 us (11%)
  starting transfers between devices  20.4 us (7%)
  between operations  14.5 us (5%)
    all_gather x2, waiting for transfers between devices, entering(): gathered = lax.all_gather(part, axis)  110 us
    add x31, other arithmetic, add_states(): return earlier + later  31.3 us
    dot_general x24, matrix products, contract(): lax.dot_general(left, right, (((left_dim,), (right_dim,)), ((), ())), pre...  23.9 us
    unnamed x50, local copies, waits for them, and re-layouts  14 us
    all_to_all x1, waiting for transfers between devices, on_device(): lax.all_to_all(key_rows, 'head', split_axis=1, concat_axis=0, tiled=True)  13.8 us
    all_to_all x1, waiting for transfers between devices, on_device(): lax.all_to_all(queries, 'head', split_axis=1, concat_axis=0, tiled=True)  12.9 us
    all_to_all x1, waiting for transfers between devices, on_device(): lax.all_to_all(value_rows, 'head', split_axis=1, concat_axis=0, tiled=True)  11.9 us
    all_to_all x1, waiting for transfers between devices, on_device(): lax.all_to_all(out_grad, 'head', split_axis=1, concat_axis=0, tiled=True)  11.3 us
  transfers between devices with their start and end apart: 6, of which 6 were waited for; matrix products, arithmetic and copies ran while one was open for 18% of the time, Pallas kernels for 0%

commit v1 on v0

v1 whole, which is shorter than its diff:
```python
import math

import jax
import jax.numpy as jnp
from jax import lax
from jax.experimental import pallas as pl
from jax.experimental.pallas import tpu as pltpu
from jax.sharding import PartitionSpec as P

HD = 128
NX, NZ, NY = 4, 8, 4
SUB = 256
MESH = pl.DeviceIdType.MESH
F32 = jnp.float32
BF16 = jnp.bfloat16
HOPS = (1, 3, 2)


def mm(left, right, left_dim, right_dim):
    return lax.dot_general(
        left, right, (((left_dim,), (right_dim,)), ((), ())), preferred_element_type=F32
    )


def kernel(
    scale, q, k, v, g, o0, o1, o2, o3,
    recv, own, acc, sib_out, sib_in, early_out, early, subs, states, pin, totals, pout, entering,
    at_sub, raw_send, raw_recv, own_sem, sib_send, sib_recv, early_send, early_recv,
    scan_send, scan_recv, up_sem,
):
    inputs = (q, k, v, g)
    outputs = (o0, o1, o2, o3)
    ctx = lax.axis_index("ctx")
    head = lax.axis_index("head")
    x, z = ctx // NZ, ctx % NZ
    y, core = head // 2, head % 2
    sibling = y * 2 + (1 - core)

    barrier = pltpu.get_barrier_semaphore()
    for d in range(1, 8):
        pl.semaphore_signal(barrier, inc=1, device_id=(ctx, (head + d) % 8), device_id_type=MESH)
    for d in range(1, NX):
        pl.semaphore_signal(barrier, inc=1, device_id=((x + d) % NX * NZ + z, head), device_id_type=MESH)

    def greet(later, carry):
        pl.semaphore_signal(barrier, inc=1, device_id=(x * NZ + later, head), device_id_type=MESH)
        return carry

    lax.fori_loop(z + 1, NZ, greet, 0)
    for a in range(4):
        pltpu.make_async_copy(inputs[a], own.at[a], own_sem).start()
    pl.semaphore_wait(barrier, 7 + NX - 1 + z)

    def answer(earlier, carry):
        pl.semaphore_signal(up_sem, inc=1, device_id=(x * NZ + earlier, head), device_id_type=MESH)
        return carry

    lax.fori_loop(0, z, answer, 0)

    def raw(h, dy, dc, a):
        to = (y + dy) % NY * 2 + (core + dc) % 2
        pltpu.make_async_remote_copy(
            src_ref=inputs[a].at[:, pl.ds(pl.multiple_of(to * 512 + h * HD, HD), HD)],
            dst_ref=recv.at[a, h, pl.ds(pl.multiple_of(head * HD, HD), HD), :],
            send_sem=raw_send,
            recv_sem=raw_recv.at[h, (NY - dy) % NY],
            device_id=(ctx, to),
            device_id_type=MESH,
        ).start()

    def send_head(h):
        for a in range(4):
            pltpu.make_async_copy(
                inputs[a].at[:, pl.ds(pl.multiple_of(head * 512 + h * HD, HD), HD)],
                recv.at[a, h, pl.ds(pl.multiple_of(head * HD, HD), HD), :],
                raw_recv.at[h, 0],
            ).start()
            raw(h, 0, 1, a)
        for dy in HOPS:
            for dc in range(2):
                for a in range(4):
                    raw(h, dy, dc, a)

    send_head(0)

    for a in range(4):
        pltpu.make_async_copy(inputs[a], own.at[a], own_sem).wait()

    def partial(dest, st):
        cols = pl.ds(pl.multiple_of(dest * 512 + 256 + st // 2 * HD, HD), HD)
        if st % 2 == 0:
            return mm(own[1, :, cols], own[2, :, cols], 0, 0)
        return mm(own[0, :, cols], own[3, :, cols], 0, 0)

    for n, dy in enumerate(HOPS + (0,)):
        to_y = (y + dy) % NY
        for st in range(4):
            sib_out[n, st] = partial(to_y * 2 + 1 - core, st)
        pltpu.make_async_remote_copy(
            src_ref=sib_out.at[n],
            dst_ref=sib_in.at[n],
            send_sem=sib_send,
            recv_sem=sib_recv.at[n],
            device_id=(ctx, sibling),
            device_id_type=MESH,
        ).start()
    for n, dy in enumerate(HOPS + (0,)):
        pltpu.make_async_copy(sib_in.at[n], sib_in.at[n], sib_recv.at[n]).wait()
        to = (y + dy) % NY * 2 + core
        for st in range(4):
            both = (partial(to, st) + sib_in[n, st]).astype(BF16)
            if dy == 0:
                early[y, st] = both
            else:
                early_out[n, st] = both
        if dy != 0:
            pltpu.make_async_remote_copy(
                src_ref=early_out.at[n],
                dst_ref=early.at[y],
                send_sem=early_send,
                recv_sem=early_recv,
                device_id=(ctx, to),
                device_id_type=MESH,
            ).start()

    def send_rest(h, carry):
        send_head(h)
        return carry

    lax.fori_loop(1, 4, send_rest, 0)

    row = lax.broadcasted_iota(jnp.int32, (SUB, SUB), 0)
    col = lax.broadcasted_iota(jnp.int32, (SUB, SUB), 1)
    causal = row >= col

    def load(h, i):
        return tuple(recv[a, h, pl.ds(pl.multiple_of(i * SUB, SUB), SUB), :] for a in range(4))

    def within(qs, ks, vs, gs):
        attn = jnp.where(causal, mm(qs, ks, 1, 1), 0.0).astype(BF16)
        back = jnp.where(causal, mm(gs, vs, 1, 1), 0.0).astype(BF16)
        return mm(attn, vs, 1, 0), mm(back, ks, 1, 0), mm(back, qs, 0, 0), mm(attn, gs, 0, 0)

    def across(qs, ks, vs, gs, pre, suf):
        return mm(qs, pre, 1, 0), mm(gs, pre, 1, 1), mm(vs, suf, 1, 1), mm(ks, suf, 1, 0)

    def arrive(h, m):
        j = m + m // 2 - 2 * (m // 3)
        i = (y + j) % NY
        landed = recv.at[:, h, pl.ds(pl.multiple_of(i * SUB, SUB), SUB), :]
        pltpu.make_async_copy(landed, landed, raw_recv.at[h, j]).wait()
        return i

    def first_heads(h):
        def one(m, carry):
            i = arrive(h, m)
            parts = load(h, i)
            qs, ks, vs, gs = parts
            subs[i, 2 * h] = mm(ks, vs, 0, 0)
            subs[i, 2 * h + 1] = mm(qs, gs, 0, 0)
            rows = pl.ds(pl.multiple_of(i * SUB, SUB), SUB)
            for n, part in enumerate(within(*parts)):
                acc[n, h, rows, :] = part
            return carry

        lax.fori_loop(0, NY, one, 0)
        for st in (2 * h, 2 * h + 1):
            total = subs[0, st] + subs[1, st] + subs[2, st] + subs[3, st]
            states[1, pl.ds(st * HD, HD), :] = total.astype(BF16)

    def store(h, i, values):
        rows = pl.ds(pl.multiple_of(i * SUB, SUB), SUB)
        for ref, value in zip(outputs, values):
            ref[rows, pl.ds(h * HD, HD)] = (value * scale).astype(BF16)

    def last_heads(h, low, high):
        def one(m, carry):
            i = arrive(h, m)
            parts = load(h, i)
            st = 2 * (h - 2)
            far = across(*parts, at_sub[0, i, st], at_sub[0, i, st + 1])
            store(h, i, [near + more for near, more in zip(within(*parts), far)])
            return carry

        lax.fori_loop(low, high, one, 0)

    def finish(h):
        def one(i, carry):
            rows = pl.ds(pl.multiple_of(i * SUB, SUB), SUB)
            far = across(*load(h, i), at_sub[1, i, 2 * h], at_sub[1, i, 2 * h + 1])
            store(h, i, [acc[n, h, rows, :] + more for n, more in enumerate(far)])
            return carry

        lax.fori_loop(0, NY, one, 0)

    ahead = z % 4 < 2
    far_first = (4, 3, 5, 2, 6, 1, 7)

    def scan_one(n):
        pin[n, z] = states[n, pl.ds(pl.multiple_of(z * 64, 64), 64), :]
        for dz in far_first:
            to = (z + dz) % NZ
            pltpu.make_async_remote_copy(
                src_ref=states.at[n, pl.ds(pl.multiple_of(to * 64, 64), 64), :],
                dst_ref=pin.at[n, z],
                send_sem=scan_send.at[n, 0],
                recv_sem=scan_recv.at[n, 0],
                device_id=(x * NZ + to, head),
                device_id_type=MESH,
            ).start()

    def scan_two(n):
        landed = pin.at[n, pl.ds(0, NZ - 1)]
        pltpu.make_async_copy(landed, landed, scan_recv.at[n, 0]).wait()
        total = pin[n, 0].astype(F32)
        for i in range(1, NZ):
            total = total + pin[n, i].astype(F32)
        totals[n, x] = total
        for dx in (2, 1, 3):
            pltpu.make_async_remote_copy(
                src_ref=totals.at[n, x],
                dst_ref=totals.at[n, x],
                send_sem=scan_send.at[n, 1],
                recv_sem=scan_recv.at[n, 1],
                device_id=((x + dx) % NX * NZ + z, head),
                device_id_type=MESH,
            ).start()

    def scan_three(n):
        landed = totals.at[n, pl.ds(0, NX - 1)]
        pltpu.make_async_copy(landed, landed, scan_recv.at[n, 1]).wait()
        base = jnp.zeros((64, HD), F32)
        for i in range(NX):
            counts = jnp.logical_or(jnp.logical_and(ahead, i < x), jnp.logical_and(jnp.logical_not(ahead), i > x))
            base = base + jnp.where(counts, totals[n, i], 0.0)
        total = totals[n, x]
        before = jnp.zeros((64, HD), F32)
        for i in range(NZ):
            mine = pin[n, i].astype(F32)
            part = jnp.where(ahead, before, total - before - mine)
            pout[n, i] = (base + part).astype(BF16)
            before = before + mine
        entering[n, pl.ds(pl.multiple_of(z * 64, 64), 64), :] = pout[n, z]
        for dz in far_first:
            to = (z + dz) % NZ
            pltpu.make_async_remote_copy(
                src_ref=pout.at[n, to],
                dst_ref=entering.at[n, pl.ds(pl.multiple_of(z * 64, 64), 64), :],
                send_sem=scan_send.at[n, 2],
                recv_sem=scan_recv.at[n, 2],
                device_id=(x * NZ + to, head),
                device_id_type=MESH,
            ).start()

    def scan_end(n):
        landed = pout.at[n, pl.ds(0, NZ - 1)]
        pltpu.make_async_copy(landed, landed, scan_recv.at[n, 2]).wait()
        for st in range(4):
            state = entering[n, pl.ds(st * HD, HD), :].astype(F32)
            for i in range(NY) if st % 2 == 0 else reversed(range(NY)):
                at_sub[n, i, st] = state.astype(BF16)
                sub = early[i, st].astype(F32) if n == 0 else subs[i, st]
                state = state + sub

    first_heads(0)

    landed = early_out.at[pl.ds(0, 3)]
    pltpu.make_async_copy(landed, landed, early_recv).wait()
    for st in range(4):
        total = early[0, st].astype(F32)
        for i in range(1, NY):
            total = total + early[i, st].astype(F32)
        states[0, pl.ds(st * HD, HD), :] = total.astype(BF16)

    @pl.when(z < NZ - 1)
    def _():
        pl.semaphore_wait(up_sem, NZ - 1 - z)

    scan_one(0)

    first_heads(1)
    scan_one(1)
    scan_two(0)
    scan_three(0)
    scan_two(1)
    scan_three(1)
    scan_end(0)
    last_heads(2, 0, 4)
    last_heads(3, 0, 3)
    scan_end(1)
    finish(0)
    finish(1)
    last_heads(3, 3, 4)

    sent = recv.at[:, :, pl.ds(0, 896), :]
    pltpu.make_async_copy(sent, sent, raw_send).wait()
    pltpu.make_async_copy(sib_out, sib_out, sib_send).wait()
    sent = early_out.at[pl.ds(0, 3)]
    pltpu.make_async_copy(sent, sent, early_send).wait()
    for n in range(2):
        sent = pout.at[n, pl.ds(0, NZ - 1)]
        pltpu.make_async_copy(sent, sent, scan_send.at[n, 0]).wait()
        pltpu.make_async_copy(sent, sent, scan_send.at[n, 2]).wait()
        sent = totals.at[n, pl.ds(0, NX - 1)]
        pltpu.make_async_copy(sent, sent, scan_send.at[n, 1]).wait()


def on_device(queries, key_rows, value_rows, out_grad):
    def body(*refs):
        kernel(1.0 / math.sqrt(4194304), *refs)

    dma = pltpu.SemaphoreType.DMA
    return pl.pallas_call(
        body,
        out_shape=[pltpu.VMEM((1024, 512), BF16)] * 4,
        in_specs=[pl.BlockSpec(memory_space=pl.ANY)] * 4,
        out_specs=[pl.BlockSpec(memory_space=pltpu.VMEM)] * 4,
        scratch_shapes=[
            pltpu.VMEM((4, 4, 1024, HD), BF16),
            pltpu.VMEM((4, 128, 4096), BF16),
            pltpu.VMEM((4, 2, 1024, HD), F32),
            pltpu.VMEM((4, 4, HD, HD), F32),
            pltpu.VMEM((4, 4, HD, HD), F32),
            pltpu.VMEM((4, 4, HD, HD), BF16),
            pltpu.VMEM((4, 4, HD, HD), BF16),
            pltpu.VMEM((4, 4, HD, HD), F32),
            pltpu.VMEM((2, 512, HD), BF16),
            pltpu.VMEM((2, NZ, 64, HD), BF16),
            pltpu.VMEM((2, NX, 64, HD), F32),
            pltpu.VMEM((2, NZ, 64, HD), BF16),
            pltpu.VMEM((2, 512, HD), BF16),
            pltpu.VMEM((2, 4, 4, HD, HD), BF16),
            dma,
            dma((4, 4)),
            dma,
            dma,
            dma((4,)),
            dma,
            dma,
            dma((2, 3)),
            dma((2, 3)),
            pltpu.SemaphoreType.REGULAR,
        ],
        compiler_params=pltpu.CompilerParams(
            collective_id=0, has_side_effects=True, vmem_limit_bytes=58 * 2**20
        ),
        name="linear_attention",
    )(queries, key_rows, value_rows, out_grad)


def solution(mesh):
    return jax.shard_map(
        on_device,
        mesh=mesh,
        in_specs=(P(("ctx", "head"), None),) * 4,
        out_specs=(P("ctx", "head"),) * 4,
        check_vma=False,
    )
```

time: 312 us -> 64.1 us (0.21)
  waiting for transfers between devices: 160 us -> 0 us
  Pallas kernels: 0 us -> 59.5 us
  matrix products: 46.6 us -> 0 us
  other arithmetic: 32.8 us -> 0 us
  local copies, waits for them, and re-layouts: 36.1 us -> 3.88 us
  starting transfers between devices: 20.4 us -> 0 us
  between operations: 14.5 us -> 0.64 us
    all_gather x2 -> x0, waiting for transfers between devices: 110 us -> none  [entering(): gathered = lax.all_gather(part, axis)]
    pallas_call x0 -> x1, Pallas kernels: none -> 59.5 us  [on_device(): pl.pallas_call(body, out_shape=[pltpu.VMEM((1024, 512), BF16)] * 4, in_sp...]
    all_to_all x4 -> x0, waiting for transfers between devices: 49.9 us -> none  [the longest x1 13.8 us: on_device(): lax.all_to_all(key_rows, 'head', split_axis=1, concat_axis=0, tiled=True)]
    dot_general x42 -> x0, matrix products: 46.6 us -> none  [the longest x24 23.9 us: contract(): lax.dot_general(left, right, (((left_dim,), (right_dim,)), ((), ())), pre...]
    add x31 -> x0, other arithmetic: 31.3 us -> none  [add_states(): return earlier + later]
    all_to_all x4 -> x0, starting transfers between devices: 20.4 us -> none  [the longest x1 6.7 us: on_device(): lax.all_to_all(key_rows, 'head', split_axis=1, concat_axis=0, tiled=True)]
    all_to_all x8 -> x0, local copies, waits for them, and re-layouts: 13.7 us -> none  [the longest x2 4.62 us: on_device(): lax.all_to_all(out_grad, 'head', split_axis=1, concat_axis=0, tiled=True)]
    unnamed x50 -> x4, local copies, waits for them, and re-layouts: 14 us -> 3.88 us
  transfers between devices with their start and end apart: 6 -> 0, of which waited for: 6 -> 0; matrix products, arithmetic and copies ran while one was open for 18% -> 0% of each run, Pallas kernels for 0% -> 0%
where the time goes in v1:
time: 64.1 us; the launch traced here: 64 us
  Pallas kernels  59.5 us (93%)
  local copies, waits for them, and re-layouts  3.88 us (6%)
    pallas_call x1, Pallas kernels, on_device(): pl.pallas_call(body, out_shape=[pltpu.VMEM((1024, 512), BF16)] * 4, in_sp...  59.5 us
    unnamed x4, local copies, waits for them, and re-layouts  3.88 us

profile of v1, /device:TPU:1, one launch (start us, length us, event | category | flops | bytes accessed | tf_op | source)
XLA Modules:
  0.0 64.0 jit_solution(12406075629477891343)
XLA Ops:
  0.6 59.5 %linear_attention.1 = (bf16[1024,512]{1,0:T(8,128)(2,1)S(1)}, bf16[1024,512]{1,0:T(8,128)(2,1)S(1)}, bf16[1024,512]{1,0:T(8,128)(2,1)S(1)}, bf16[1024,512]{1,0:T(8,128)(2,1)S(1)}) custom-call(bf16[128,4096]{1,0:T(8,128)(2,1)} %refs_0_.1, bf16[128,4096]{1,0:T(8,128)(2,1)} %refs_1_.1, bf16[128,4096]{1,0:T(8,128)(2,1)} %refs_2_.1, bf16[128,4096]{1,0:T(8,128)(2,1)} %refs_3_.1), custom_call_target="tpu_custom_call" | custom-call | tf_op jit(solution)/shard_map/linear_attention/pallas_call | solution.py:313
  60.2 1.0 %copy.12 = bf16[1024,512]{1,0:T(8,128)(2,1)} copy(bf16[1024,512]{1,0:T(8,128)(2,1)S(1)} %get-tuple-element.4) | data formatting | bytes 2097152
  61.1 1.0 %copy.13 = bf16[1024,512]{1,0:T(8,128)(2,1)} copy(bf16[1024,512]{1,0:T(8,128)(2,1)S(1)} %get-tuple-element.5) | data formatting | bytes 2097152
  62.1 1.0 %copy.14 = bf16[1024,512]{1,0:T(8,128)(2,1)} copy(bf16[1024,512]{1,0:T(8,128)(2,1)S(1)} %get-tuple-element.6) | data formatting | bytes 2097152
  63.1 1.0 %copy.15 = bf16[1024,512]{1,0:T(8,128)(2,1)} copy(bf16[1024,512]{1,0:T(8,128)(2,1)S(1)} %get-tuple-element.7) | data formatting | bytes 2097152

commit v2 on v1

v2 whole, which is shorter than its diff:
```python
import math

import jax
import jax.numpy as jnp
from jax import lax
from jax.experimental import pallas as pl
from jax.experimental.pallas import tpu as pltpu
from jax.sharding import PartitionSpec as P

HD = 128
NX, NZ, NY = 4, 8, 4
SUB = 256
SLICE = 2 * HD // NZ
VMEM_LIMIT = 58 * 2**20
MESH = pl.DeviceIdType.MESH
F32 = jnp.float32
BF16 = jnp.bfloat16


def mm(left, right, left_dim, right_dim):
    return lax.dot_general(
        left, right, (((left_dim,), (right_dim,)), ((), ())), preferred_element_type=F32
    )


def kernel(
    scale, q, k, v, g, o0, o1, o2, o3,
    recv, own, acc, sib_out, sib_in, early_out, early_in, onward, subs, states, pin, totals, pout,
    entering, inner, raw_send, raw_recv, own_sem, sib_send, sib_recv, early_send, early_recv,
    scan_send, scan_recv, up_sem,
):
    inputs = (q, k, v, g)
    outputs = (o0, o1, o2, o3)
    ctx = lax.axis_index("ctx")
    head = lax.axis_index("head")
    x, z = ctx // NZ, ctx % NZ
    y, core = head // 2, head % 2
    sibling = y * 2 + (1 - core)

    barrier = pltpu.get_barrier_semaphore()
    for d in range(1, 8):
        pl.semaphore_signal(barrier, inc=1, device_id=(ctx, (head + d) % 8), device_id_type=MESH)

    def greet_x(later, carry):
        pl.semaphore_signal(barrier, inc=1, device_id=(later * NZ + z, head), device_id_type=MESH)
        return carry

    def greet_z(later, carry):
        pl.semaphore_signal(barrier, inc=1, device_id=(x * NZ + later, head), device_id_type=MESH)
        return carry

    lax.fori_loop(x + 1, NX, greet_x, 0)
    lax.fori_loop(z + 1, NZ, greet_z, 0)
    for a in range(4):
        pltpu.make_async_copy(inputs[a], own.at[a], own_sem).start()
    pl.semaphore_wait(barrier, 7 + x + z)

    def answer_x(earlier, carry):
        pl.semaphore_signal(up_sem, inc=1, device_id=(earlier * NZ + z, head), device_id_type=MESH)
        return carry

    def answer_z(earlier, carry):
        pl.semaphore_signal(up_sem, inc=1, device_id=(x * NZ + earlier, head), device_id_type=MESH)
        return carry

    lax.fori_loop(0, x, answer_x, 0)
    lax.fori_loop(0, z, answer_z, 0)

    def raw(h, dy, dc, a):
        to = (y + dy) % NY * 2 + (core + dc) % 2
        return pltpu.make_async_remote_copy(
            src_ref=inputs[a].at[:, pl.ds(pl.multiple_of(to * 512 + h * HD, HD), HD)],
            dst_ref=recv.at[a, h, pl.ds(pl.multiple_of(head * HD, HD), HD), :],
            send_sem=raw_send,
            recv_sem=raw_recv.at[h, (NY - dy) % NY],
            device_id=(ctx, to),
            device_id_type=MESH,
        )

    peers = [(0, 1)] + [(dy, dc) for dy in (1, 3, 2) for dc in range(2)]

    def keep(h, arrays):
        for a in arrays:
            pltpu.make_async_copy(
                inputs[a].at[:, pl.ds(pl.multiple_of(head * 512 + h * HD, HD), HD)],
                recv.at[a, h, pl.ds(pl.multiple_of(head * HD, HD), HD), :],
                raw_recv.at[h, 0],
            ).start()

    def send(h, arrays):
        for dy, dc in peers:
            for a in arrays:
                raw(h, dy, dc, a).start()

    keep(0, range(4))
    send(0, range(4))

    up = 1 + 2 * core
    down = 3 - 2 * core
    for a in range(4):
        pltpu.make_async_copy(inputs[a], own.at[a], own_sem).wait()

    def partial(dest, st):
        cols = pl.ds(pl.multiple_of(dest * 512 + 256 + st // 2 * HD, HD), HD)
        if st % 2 == 0:
            return mm(own[1, :, cols], own[2, :, cols], 0, 0)
        return mm(own[0, :, cols], own[3, :, cols], 0, 0)

    for n, dy in enumerate((2, up, down, 0)):
        for st in range(4):
            sib_out[n, st] = partial((y + dy) % NY * 2 + 1 - core, st)
        place = (0, 2, 1, 3)[n]
        pltpu.make_async_remote_copy(
            src_ref=sib_out.at[n],
            dst_ref=sib_in.at[place],
            send_sem=sib_send,
            recv_sem=sib_recv.at[place],
            device_id=(ctx, sibling),
            device_id_type=MESH,
        ).start()

    def send_early(n, dy):
        pltpu.make_async_remote_copy(
            src_ref=early_out.at[n],
            dst_ref=early_in.at[n],
            send_sem=early_send,
            recv_sem=early_recv.at[n],
            device_id=(ctx, (y + dy) % NY * 2 + core),
            device_id_type=MESH,
        ).start()

    for n, dy in ((0, 2), (2, down), (1, up), (3, 0)):
        pltpu.make_async_copy(sib_in.at[n], sib_in.at[n], sib_recv.at[n]).wait()
        for st in range(4):
            both = partial((y + dy) % NY * 2 + core, st) + sib_in[n, st]
            if n == 3:
                subs[2 + st // 2, y, st % 2] = both
            elif n == 1:
                onward[st] = both
            else:
                early_out[n, st] = both.astype(BF16)
        if n == 0:
            send_early(0, up)
        if n == 2:
            send_early(2, down)

    keep(1, range(4))
    send(1, (1, 2))
    pltpu.make_async_copy(early_in.at[0], early_in.at[0], early_recv.at[0]).wait()
    for st in range(4):
        early_out[1, st] = (onward[st] + early_in[0, st].astype(F32)).astype(BF16)
    send_early(1, up)
    send(1, (0, 3))

    def send_rest(h, carry):
        keep(h, range(4))
        send(h, range(4))
        return carry

    lax.fori_loop(2, 4, send_rest, 0)

    row = lax.broadcasted_iota(jnp.int32, (SUB, SUB), 0)
    col = lax.broadcasted_iota(jnp.int32, (SUB, SUB), 1)
    causal = row >= col

    def load(h, i):
        return tuple(recv[a, h, pl.ds(pl.multiple_of(i * SUB, SUB), SUB), :] for a in range(4))

    def within(qs, ks, vs, gs):
        attn = jnp.where(causal, mm(qs, ks, 1, 1), 0.0).astype(BF16)
        back = jnp.where(causal, mm(gs, vs, 1, 1), 0.0).astype(BF16)
        return mm(attn, vs, 1, 0), mm(back, ks, 1, 0), mm(back, qs, 0, 0), mm(attn, gs, 0, 0)

    def across(h, i, qs, ks, vs, gs):
        pre, suf = entering[h, 0:HD, :], entering[h, HD : 2 * HD, :]
        pre_in, suf_in = inner[h, i, 0], inner[h, i, 1]

        def twice(rows):
            return jnp.concatenate([rows, rows], axis=1)

        pre_rows, pre_cols = jnp.concatenate([pre, pre_in], axis=0), jnp.concatenate([pre, pre_in], axis=1)
        suf_rows, suf_cols = jnp.concatenate([suf, suf_in], axis=0), jnp.concatenate([suf, suf_in], axis=1)
        return (
            mm(twice(qs), pre_rows, 1, 0),
            mm(twice(gs), pre_cols, 1, 1),
            mm(twice(vs), suf_cols, 1, 1),
            mm(twice(ks), suf_rows, 1, 0),
        )

    def arrive(h, j):
        i = (y + j) % NY
        landed = recv.at[:, h, pl.ds(pl.multiple_of(i * SUB, SUB), SUB), :]
        pltpu.make_async_copy(landed, landed, raw_recv.at[h, j]).wait()
        return i

    def first_heads(h, low, high):
        def one(m, carry):
            i = arrive(h, m + m // 2 - 2 * (m // 3))
            parts = load(h, i)
            qs, ks, vs, gs = parts
            subs[h, i, 0] = mm(ks, vs, 0, 0)
            subs[h, i, 1] = mm(qs, gs, 0, 0)
            rows = pl.ds(pl.multiple_of(i * SUB, SUB), SUB)
            for n, part in enumerate(within(*parts)):
                acc[n, h, rows, :] = part
            return carry

        lax.fori_loop(low, high, one, 0)

    def store(h, i, values):
        rows = pl.ds(pl.multiple_of(i * SUB, SUB), SUB)
        for ref, value in zip(outputs, values):
            ref[rows, pl.ds(h * HD, HD)] = (value * scale).astype(BF16)

    def whole(h, i):
        parts = load(h, i)
        far = across(h, i, *parts)
        store(h, i, [near + more for near, more in zip(within(*parts), far)])

    def last_heads(h):
        for j in (0, 1, 3):
            arrive(h, j)
        before = (y + down) % NY
        qs, ks, vs, gs = load(h, before)
        for st, state in enumerate((mm(ks, vs, 0, 0), mm(qs, gs, 0, 0))):
            place = 2 * (h - 2) + st
            subs[h, (y + up) % NY, st] = early_in[2, place].astype(F32)
            subs[h, before, st] = state
            subs[h, (y + 2) % NY, st] = early_in[1, place].astype(F32) - state
        inner_states(h)

        def one(m, carry):
            whole(h, (y + m + m // 2) % NY)
            return carry

        lax.fori_loop(0, 3, one, 0)

    def finish(h):
        def one(i, carry):
            rows = pl.ds(pl.multiple_of(i * SUB, SUB), SUB)
            far = across(h, i, *load(h, i))
            store(h, i, [acc[n, h, rows, :] + more for n, more in enumerate(far)])
            return carry

        lax.fori_loop(0, NY, one, 0)

    def inner_states(h):
        for st in range(2):
            state = jnp.zeros((HD, HD), F32)
            for i in range(NY) if st == 0 else reversed(range(NY)):
                inner[h, i, st] = state.astype(BF16)
                state = state + subs[h, i, st]

    def block_states(h):
        for st in range(2):
            if h < 2:
                total = subs[h, 0, st] + subs[h, 1, st] + subs[h, 2, st] + subs[h, 3, st]
            else:
                place = 2 * (h - 2) + st
                total = subs[h, y, st] + early_in[1, place].astype(F32) + early_in[2, place].astype(F32)
            states[h, pl.ds(st * HD, HD), :] = total.astype(BF16)

    ahead = z < NZ // 2
    far_first = (4, 3, 5, 2, 6, 1, 7)

    def slice_of(place):
        return pl.ds(pl.multiple_of(place * SLICE, SLICE), SLICE)

    def scan_one(h):
        pin[h, z] = states[h, slice_of(z), :]
        for dz in far_first:
            to = (z + dz) % NZ
            pltpu.make_async_remote_copy(
                src_ref=states.at[h, slice_of(to), :],
                dst_ref=pin.at[h, z],
                send_sem=scan_send.at[h, 0],
                recv_sem=scan_recv.at[h, 0],
                device_id=(x * NZ + to, head),
                device_id_type=MESH,
            ).start()

    def scan_two(h):
        landed = pin.at[h, pl.ds(0, NZ - 1)]
        pltpu.make_async_copy(landed, landed, scan_recv.at[h, 0]).wait()
        total = pin[h, 0].astype(F32)
        for i in range(1, NZ):
            total = total + pin[h, i].astype(F32)
        totals[h, x] = total
        for dx in (2, 1, 3):
            pltpu.make_async_remote_copy(
                src_ref=totals.at[h, x],
                dst_ref=totals.at[h, x],
                send_sem=scan_send.at[h, 1],
                recv_sem=scan_recv.at[h, 1],
                device_id=((x + dx) % NX * NZ + z, head),
                device_id_type=MESH,
            ).start()

    def scan_three(h):
        landed = totals.at[h, pl.ds(0, NX - 1)]
        pltpu.make_async_copy(landed, landed, scan_recv.at[h, 1]).wait()
        base = jnp.zeros((SLICE, HD), F32)
        for i in range(NX):
            counts = jnp.logical_or(jnp.logical_and(ahead, i < x), jnp.logical_and(jnp.logical_not(ahead), i > x))
            base = base + jnp.where(counts, totals[h, i], 0.0)
        total = totals[h, x]
        before = jnp.zeros((SLICE, HD), F32)
        for i in range(NZ):
            mine = pin[h, i].astype(F32)
            part = jnp.where(ahead, before, total - before - mine)
            pout[h, i] = (base + part).astype(BF16)
            before = before + mine
        entering[h, slice_of(z), :] = pout[h, z]
        for dz in far_first:
            to = (z + dz) % NZ
            pltpu.make_async_remote_copy(
                src_ref=pout.at[h, to],
                dst_ref=entering.at[h, slice_of(z), :],
                send_sem=scan_send.at[h, 2],
                recv_sem=scan_recv.at[h, 2],
                device_id=(x * NZ + to, head),
                device_id_type=MESH,
            ).start()

    def scan_end(h):
        landed = pout.at[h, pl.ds(0, NZ - 1)]
        pltpu.make_async_copy(landed, landed, scan_recv.at[h, 2]).wait()

    first_heads(0, 0, 4)
    block_states(0)
    later = NX - 1 - x + NZ - 1 - z

    @pl.when(later > 0)
    def _():
        pl.semaphore_wait(up_sem, later)

    scan_one(0)
    for n in (1, 2):
        pltpu.make_async_copy(early_in.at[n], early_in.at[n], early_recv.at[n]).wait()
    for h in (2, 3):
        block_states(h)
        scan_one(h)
    first_heads(1, 0, 3)
    for h in (0, 2, 3):
        scan_two(h)
    first_heads(1, 3, 4)
    block_states(1)
    scan_one(1)
    for h in (0, 2, 3):
        scan_three(h)
    inner_states(0)
    inner_states(1)
    scan_two(1)
    scan_three(1)
    scan_end(2)
    last_heads(2)
    whole(2, arrive(2, 2))
    scan_end(3)
    scan_end(0)
    finish(0)
    scan_end(1)
    finish(1)
    last_heads(3)
    whole(3, arrive(3, 2))

    sent = recv.at[:, :, pl.ds(0, 896), :]
    pltpu.make_async_copy(sent, sent, raw_send).wait()
    pltpu.make_async_copy(sib_out, sib_out, sib_send).wait()
    sent = early_in
    pltpu.make_async_copy(sent, sent, early_send).wait()
    for n in range(4):
        sent = pout.at[n, pl.ds(0, NZ - 1)]
        pltpu.make_async_copy(sent, sent, scan_send.at[n, 0]).wait()
        pltpu.make_async_copy(sent, sent, scan_send.at[n, 2]).wait()
        sent = totals.at[n, pl.ds(0, NX - 1)]
        pltpu.make_async_copy(sent, sent, scan_send.at[n, 1]).wait()


def write_out(a, b, c, d, out_a, out_b, out_c, out_d, sem):
    pairs = ((a, out_a), (b, out_b), (c, out_c), (d, out_d))
    for src, dst in pairs:
        pltpu.make_async_copy(src, dst, sem).start()
    for src, dst in pairs:
        pltpu.make_async_copy(src, dst, sem).wait()


def on_device(queries, key_rows, value_rows, out_grad):
    def body(*refs):
        kernel(1.0 / math.sqrt(4194304), *refs)

    dma = pltpu.SemaphoreType.DMA
    results = pl.pallas_call(
        body,
        out_shape=[pltpu.VMEM((1024, 512), BF16)] * 4,
        in_specs=[pl.BlockSpec(memory_space=pl.ANY)] * 4,
        out_specs=[pl.BlockSpec(memory_space=pltpu.VMEM)] * 4,
        scratch_shapes=[
            pltpu.VMEM((4, 4, 1024, HD), BF16),
            pltpu.VMEM((4, 128, 4096), BF16),
            pltpu.VMEM((4, 2, 1024, HD), F32),
            pltpu.VMEM((4, 4, HD, HD), F32),
            pltpu.VMEM((4, 4, HD, HD), F32),
            pltpu.VMEM((3, 4, HD, HD), BF16),
            pltpu.VMEM((3, 4, HD, HD), BF16),
            pltpu.VMEM((4, HD, HD), F32),
            pltpu.VMEM((4, 4, 2, HD, HD), F32),
            pltpu.VMEM((4, 2 * HD, HD), BF16),
            pltpu.VMEM((4, NZ, SLICE, HD), BF16),
            pltpu.VMEM((4, NX, SLICE, HD), F32),
            pltpu.VMEM((4, NZ, SLICE, HD), BF16),
            pltpu.VMEM((4, 2 * HD, HD), BF16),
            pltpu.VMEM((4, 4, 2, HD, HD), BF16),
            dma,
            dma((4, 4)),
            dma,
            dma,
            dma((4,)),
            dma,
            dma((3,)),
            dma((4, 3)),
            dma((4, 3)),
            pltpu.SemaphoreType.REGULAR,
        ],
        compiler_params=pltpu.CompilerParams(
            collective_id=0, has_side_effects=True, vmem_limit_bytes=VMEM_LIMIT
        ),
        name="linear_attention",
    )(queries, key_rows, value_rows, out_grad)
    return pl.pallas_call(
        write_out,
        out_shape=[pltpu.HBM((1024, 512), BF16)] * 4,
        in_specs=[pl.BlockSpec(memory_space=pltpu.VMEM)] * 4,
        out_specs=[pl.BlockSpec(memory_space=pltpu.HBM)] * 4,
        scratch_shapes=[dma],
        compiler_params=pltpu.CompilerParams(vmem_limit_bytes=VMEM_LIMIT),
        name="write_out",
    )(*[pltpu.with_memory_space_constraint(result, pltpu.VMEM) for result in results])


def solution(mesh):
    return jax.shard_map(
        on_device,
        mesh=mesh,
        in_specs=(P(("ctx", "head"), None),) * 4,
        out_specs=(P("ctx", "head"),) * 4,
        check_vma=False,
    )
```

time: 64.1 us -> 60.7 us (0.947)
  local copies, waits for them, and re-layouts: 3.88 us -> 0 us
    unnamed x4 -> x0, local copies, waits for them, and re-layouts: 3.88 us -> none
    pallas_call x0 -> x1, Pallas kernels: none -> 2.02 us  [on_device(): pl.pallas_call(write_out, out_shape=[pltpu.HBM((1024, 512), BF16)] * 4, i...]
    pallas_call x1, Pallas kernels: 59.5 us -> 57.9 us  [on_device(): pl.pallas_call(body, out_shape=[pltpu.VMEM((1024, 512), BF16)] * 4, in_sp...]
where the time goes in v2:
time: 60.7 us; the launch traced here: 60.6 us
  Pallas kernels  59.9 us (99%)
  between operations  0.64 us (1%)
    pallas_call x1, Pallas kernels, on_device(): pl.pallas_call(body, out_shape=[pltpu.VMEM((1024, 512), BF16)] * 4, in_sp...  57.9 us
    pallas_call x1, Pallas kernels, on_device(): pl.pallas_call(write_out, out_shape=[pltpu.HBM((1024, 512), BF16)] * 4, i...  2.02 us

profile of v2, /device:TPU:1, one launch (start us, length us, event | category | flops | bytes accessed | tf_op | source)
XLA Modules:
  0.0 60.6 jit_solution(16736923843491316339)
XLA Ops:
  0.6 57.9 %linear_attention.1 = (bf16[1024,512]{1,0:T(8,128)(2,1)S(1)}, bf16[1024,512]{1,0:T(8,128)(2,1)S(1)}, bf16[1024,512]{1,0:T(8,128)(2,1)S(1)}, bf16[1024,512]{1,0:T(8,128)(2,1)S(1)}) custom-call(bf16[128,4096]{1,0:T(8,128)(2,1)} %refs_0_.1, bf16[128,4096]{1,0:T(8,128)(2,1)} %refs_1_.1, bf16[128,4096]{1,0:T(8,128)(2,1)} %refs_2_.1, bf16[128,4096]{1,0:T(8,128)(2,1)} %refs_3_.1), custom_call_target="tpu_custom_call" | custom-call | tf_op jit(solution)/shard_map/linear_attention/pallas_call | solution.py:392
  58.6 2.0 %write_out.1 = (bf16[1024,512]{1,0:T(8,128)(2,1)}, bf16[1024,512]{1,0:T(8,128)(2,1)}, bf16[1024,512]{1,0:T(8,128)(2,1)}, bf16[1024,512]{1,0:T(8,128)(2,1)}) custom-call(bf16[1024,512]{1,0:T(8,128)(2,1)S(1)} %get-tuple-element.8.a, bf16[1024,512]{1,0:T(8,128)(2,1)S(1)} %get-tuple-element.9.b, bf16[1024,512]{1,0:T(8,128)(2,1)S(1)} %get-tuple-element.10.c, ...), custom_call_target="tpu_custom_call" | custom-call | tf_op jit(solution)/shard_map/write_out/pallas_call | solution.py:429

commit v3 on v2

--- a/solution.py
+++ b/solution.py
@@ -27,7 +27,7 @@
     scale, q, k, v, g, o0, o1, o2, o3,
     recv, own, acc, sib_out, sib_in, early_out, early_in, onward, subs, states, pin, totals, pout,
     entering, inner, raw_send, raw_recv, own_sem, sib_send, sib_recv, early_send, early_recv,
-    scan_send, scan_recv, up_sem,
+    scan_send, scan_recv, up_sem, first_sem,
 ):
     inputs = (q, k, v, g)
     outputs = (o0, o1, o2, o3)
@@ -38,8 +38,12 @@
     sibling = y * 2 + (1 - core)
 
     barrier = pltpu.get_barrier_semaphore()
-    for d in range(1, 8):
-        pl.semaphore_signal(barrier, inc=1, device_id=(ctx, (head + d) % 8), device_id_type=MESH)
+
+    @pl.when(head > 0)
+    def _():
+        for d in range(1, 8):
+            pl.semaphore_signal(barrier, inc=1, device_id=(ctx, (head + d) % 8), device_id_type=MESH)
+
 
     def greet_x(later, carry):
         pl.semaphore_signal(barrier, inc=1, device_id=(later * NZ + z, head), device_id_type=MESH)
@@ -53,7 +57,13 @@
     lax.fori_loop(z + 1, NZ, greet_z, 0)
     for a in range(4):
         pltpu.make_async_copy(inputs[a], own.at[a], own_sem).start()
-    pl.semaphore_wait(barrier, 7 + x + z)
+    pl.semaphore_wait(barrier, 7 - (head + 7) // 8 + x + z)
+
+    @pl.when(head == 0)
+    def _():
+        for d in range(1, 8):
+            pl.semaphore_signal(first_sem, inc=1, device_id=(ctx, d), device_id_type=MESH)
+
 
     def answer_x(earlier, carry):
         pl.semaphore_signal(up_sem, inc=1, device_id=(earlier * NZ + z, head), device_id_type=MESH)
@@ -65,6 +75,9 @@
 
     lax.fori_loop(0, x, answer_x, 0)
     lax.fori_loop(0, z, answer_z, 0)
+
+    def sem_row(h, a):
+        return 4 if isinstance(h, int) and h == 1 and a in (0, 3) else h
 
     def raw(h, dy, dc, a):
         to = (y + dy) % NY * 2 + (core + dc) % 2
@@ -72,7 +85,7 @@
             src_ref=inputs[a].at[:, pl.ds(pl.multiple_of(to * 512 + h * HD, HD), HD)],
             dst_ref=recv.at[a, h, pl.ds(pl.multiple_of(head * HD, HD), HD), :],
             send_sem=raw_send,
-            recv_sem=raw_recv.at[h, (NY - dy) % NY],
+            recv_sem=raw_recv.at[sem_row(h, a), (NY - dy) % NY],
             device_id=(ctx, to),
             device_id_type=MESH,
         )
@@ -84,7 +97,7 @@
             pltpu.make_async_copy(
                 inputs[a].at[:, pl.ds(pl.multiple_of(head * 512 + h * HD, HD), HD)],
                 recv.at[a, h, pl.ds(pl.multiple_of(head * HD, HD), HD), :],
-                raw_recv.at[h, 0],
+                raw_recv.at[sem_row(h, a), 0],
             ).start()
 
     def send(h, arrays):
@@ -92,8 +105,38 @@
             for a in arrays:
                 raw(h, dy, dc, a).start()
 
+    def raw_to(h, ty, tc):
+        to = ty * 2 + tc
+
+        @pl.when(to != head)
+        def _():
+            for a in range(4):
+                pltpu.make_async_remote_copy(
+                    src_ref=inputs[a].at[:, pl.ds(pl.multiple_of(to * 512 + h * HD, HD), HD)],
+                    dst_ref=recv.at[a, h, pl.ds(pl.multiple_of(head * HD, HD), HD), :],
+                    send_sem=raw_send,
+                    recv_sem=raw_recv.at[h, (y + NY - ty) % NY],
+                    device_id=(ctx, to),
+                    device_id_type=MESH,
+                ).start()
+
+    def send_last(h):
+        for dy in (0, 1, 3, 2):
+            for tc in (1, 0):
+                raw_to(h, (y + dy) % NY, tc)
+
     keep(0, range(4))
-    send(0, range(4))
+    for dy, dc in peers:
+
+        @pl.when((y + dy) % NY * 2 + (core + dc) % 2 > 0)
+        def _():
+            for a in range(4):
+                raw(0, dy, dc, a).start()
+
+    @pl.when(head > 0)
+    def _():
+        pl.semaphore_wait(first_sem, 1)
+        raw_to(0, 0, 0)
 
     up = 1 + 2 * core
     down = 3 - 2 * core
@@ -157,7 +200,9 @@
         send(h, range(4))
         return carry
 
-    lax.fori_loop(2, 4, send_rest, 0)
+    send_rest(2, 0)
+    keep(3, range(4))
+    send_last(3)
 
     row = lax.broadcasted_iota(jnp.int32, (SUB, SUB), 0)
     col = lax.broadcasted_iota(jnp.int32, (SUB, SUB), 1)
@@ -193,19 +238,43 @@
         pltpu.make_async_copy(landed, landed, raw_recv.at[h, j]).wait()
         return i
 
-    def first_heads(h, low, high):
+    def arrive_half(row, j):
+        i = (y + j) % NY
+        landed = recv.at[pl.ds(0, 2), 1, pl.ds(pl.multiple_of(i * SUB, SUB), SUB), :]
+        pltpu.make_async_copy(landed, landed, raw_recv.at[row, j]).wait()
+        return i
+
+    def near_parts(h, i, parts):
+        rows = pl.ds(pl.multiple_of(i * SUB, SUB), SUB)
+        for n, part in enumerate(within(*parts)):
+            acc[n, h, rows, :] = part
+
+    def head_0():
         def one(m, carry):
-            i = arrive(h, m + m // 2 - 2 * (m // 3))
-            parts = load(h, i)
+            i = arrive(0, m + m // 2 - 2 * (m // 3))
+            parts = load(0, i)
             qs, ks, vs, gs = parts
-            subs[h, i, 0] = mm(ks, vs, 0, 0)
-            subs[h, i, 1] = mm(qs, gs, 0, 0)
-            rows = pl.ds(pl.multiple_of(i * SUB, SUB), SUB)
-            for n, part in enumerate(within(*parts)):
-                acc[n, h, rows, :] = part
+            subs[0, i, 0] = mm(ks, vs, 0, 0)
+            subs[0, i, 1] = mm(qs, gs, 0, 0)
+            near_parts(0, i, parts)
             return carry
 
-        lax.fori_loop(low, high, one, 0)
+        lax.fori_loop(0, NY, one, 0)
+
+    def head_1_keys():
+        def one(m, carry):
+            i = arrive_half(1, m + m // 2 - 2 * (m // 3))
+            qs, ks, vs, gs = load(1, i)
+            subs[1, i, 0] = mm(ks, vs, 0, 0)
+            return carry
+
+        lax.fori_loop(0, NY, one, 0)
+
+    def head_1_queries(j):
+        i = arrive_half(4, j)
+        qs, ks, vs, gs = load(1, i)
+        subs[1, i, 1] = mm(qs, gs, 0, 0)
+        return i
 
     def store(h, i, values):
         rows = pl.ds(pl.multiple_of(i * SUB, SUB), SUB)
@@ -215,11 +284,19 @@
     def whole(h, i):
         parts = load(h, i)
         far = across(h, i, *parts)
-        store(h, i, [near + more for near, more in zip(within(*parts), far)])
-
-    def last_heads(h):
-        for j in (0, 1, 3):
-            arrive(h, j)
+        store(h, i, [close + more for close, more in zip(within(*parts), far)])
+
+    def whole(h, j):
+        i = arrive(h, j)
+        parts = load(h, i)
+        far = across(h, i, *parts)
+        store(h, i, [close + more for close, more in zip(within(*parts), far)])
+
+    def near(h, j):
+        i = arrive(h, j)
+        near_parts(h, i, load(h, i))
+
+    def other_states(h):
         before = (y + down) % NY
         qs, ks, vs, gs = load(h, before)
         for st, state in enumerate((mm(ks, vs, 0, 0), mm(qs, gs, 0, 0))):
@@ -229,20 +306,18 @@
             subs[h, (y + 2) % NY, st] = early_in[1, place].astype(F32) - state
         inner_states(h)
 
+    def far_parts(h, i):
+        rows = pl.ds(pl.multiple_of(i * SUB, SUB), SUB)
+        far = across(h, i, *load(h, i))
+        store(h, i, [acc[n, h, rows, :] + more for n, more in enumerate(far)])
+
+    def finish(h):
         def one(m, carry):
-            whole(h, (y + m + m // 2) % NY)
+            far_parts(h, 2 * m)
+            far_parts(h, 2 * m + 1)
             return carry
 
-        lax.fori_loop(0, 3, one, 0)
-
-    def finish(h):
-        def one(i, carry):
-            rows = pl.ds(pl.multiple_of(i * SUB, SUB), SUB)
-            far = across(h, i, *load(h, i))
-            store(h, i, [acc[n, h, rows, :] + more for n, more in enumerate(far)])
-            return carry
-
-        lax.fori_loop(0, NY, one, 0)
+        lax.fori_loop(0, NY // 2, one, 0)
 
     def inner_states(h):
         for st in range(2):
@@ -251,8 +326,8 @@
                 inner[h, i, st] = state.astype(BF16)
                 state = state + subs[h, i, st]
 
-    def block_states(h):
-        for st in range(2):
+    def block_states(h, sts=(0, 1)):
+        for st in sts:
             if h < 2:
                 total = subs[h, 0, st] + subs[h, 1, st] + subs[h, 2, st] + subs[h, 3, st]
             else:
@@ -260,73 +335,81 @@
                 total = subs[h, y, st] + early_in[1, place].astype(F32) + early_in[2, place].astype(F32)
             states[h, pl.ds(st * HD, HD), :] = total.astype(BF16)
 
-    ahead = z < NZ // 2
     far_first = (4, 3, 5, 2, 6, 1, 7)
 
-    def slice_of(place):
-        return pl.ds(pl.multiple_of(place * SLICE, SLICE), SLICE)
-
-    def scan_one(h):
-        pin[h, z] = states[h, slice_of(z), :]
-        for dz in far_first:
-            to = (z + dz) % NZ
+    class Scan:
+        def __init__(self, n, h, first, rows):
+            self.n, self.h, self.first, self.size = n, h, first, rows // NZ
+            self.ahead = (first + z * self.size) // HD == 0
+
+        def slice_of(self, place):
+            return pl.ds(pl.multiple_of(self.first + place * self.size, self.size), self.size)
+
+        def part(self, ref, place):
+            return ref.at[self.n, place, pl.ds(0, self.size), :]
+
+        def send(self, phase, src, dst, to):
             pltpu.make_async_remote_copy(
-                src_ref=states.at[h, slice_of(to), :],
-                dst_ref=pin.at[h, z],
-                send_sem=scan_send.at[h, 0],
-                recv_sem=scan_recv.at[h, 0],
-                device_id=(x * NZ + to, head),
+                src_ref=src,
+                dst_ref=dst,
+                send_sem=scan_send.at[self.n, phase],
+                recv_sem=scan_recv.at[self.n, phase],
+                device_id=(to, head),
                 device_id_type=MESH,
             ).start()
 
-    def scan_two(h):
-        landed = pin.at[h, pl.ds(0, NZ - 1)]
-        pltpu.make_async_copy(landed, landed, scan_recv.at[h, 0]).wait()
-        total = pin[h, 0].astype(F32)
-        for i in range(1, NZ):
-            total = total + pin[h, i].astype(F32)
-        totals[h, x] = total
-        for dx in (2, 1, 3):
-            pltpu.make_async_remote_copy(
-                src_ref=totals.at[h, x],
-                dst_ref=totals.at[h, x],
-                send_sem=scan_send.at[h, 1],
-                recv_sem=scan_recv.at[h, 1],
-                device_id=((x + dx) % NX * NZ + z, head),
-                device_id_type=MESH,
-            ).start()
-
-    def scan_three(h):
-        landed = totals.at[h, pl.ds(0, NX - 1)]
-        pltpu.make_async_copy(landed, landed, scan_recv.at[h, 1]).wait()
-        base = jnp.zeros((SLICE, HD), F32)
-        for i in range(NX):
-            counts = jnp.logical_or(jnp.logical_and(ahead, i < x), jnp.logical_and(jnp.logical_not(ahead), i > x))
-            base = base + jnp.where(counts, totals[h, i], 0.0)
-        total = totals[h, x]
-        before = jnp.zeros((SLICE, HD), F32)
-        for i in range(NZ):
-            mine = pin[h, i].astype(F32)
-            part = jnp.where(ahead, before, total - before - mine)
-            pout[h, i] = (base + part).astype(BF16)
-            before = before + mine
-        entering[h, slice_of(z), :] = pout[h, z]
-        for dz in far_first:
-            to = (z + dz) % NZ
-            pltpu.make_async_remote_copy(
-                src_ref=pout.at[h, to],
-                dst_ref=entering.at[h, slice_of(z), :],
-                send_sem=scan_send.at[h, 2],
-                recv_sem=scan_recv.at[h, 2],
-                device_id=(x * NZ + to, head),
-                device_id_type=MESH,
-            ).start()
-
-    def scan_end(h):
-        landed = pout.at[h, pl.ds(0, NZ - 1)]
-        pltpu.make_async_copy(landed, landed, scan_recv.at[h, 2]).wait()
-
-    first_heads(0, 0, 4)
+        def landed(self, phase, ref, count, sems):
+            copies = ref.at[self.n, pl.ds(0, count), pl.ds(0, self.size), :]
+            pltpu.make_async_copy(copies, copies, sems.at[self.n, phase]).wait()
+
+        def one(self):
+            self.part(pin, z)[...] = states[self.h, self.slice_of(z), :]
+            for dz in far_first:
+                to = (z + dz) % NZ
+                self.send(0, states.at[self.h, self.slice_of(to), :], self.part(pin, z), x * NZ + to)
+
+        def two(self):
+            self.landed(0, pin, NZ - 1, scan_recv)
+            total = self.part(pin, 0)[...].astype(F32)
+            for i in range(1, NZ):
+                total = total + self.part(pin, i)[...].astype(F32)
+            self.part(totals, x)[...] = total
+            for dx in (2, 1, 3):
+                self.send(1, self.part(totals, x), self.part(totals, x), (x + dx) % NX * NZ + z)
+
+        def three(self):
+            self.landed(1, totals, NX - 1, scan_recv)
+            base = jnp.zeros((self.size, HD), F32)
+            for i in range(NX):
+                counts = jnp.logical_or(
+                    jnp.logical_and(self.ahead, i < x),
+                    jnp.logical_and(jnp.logical_not(self.ahead), i > x),
+                )
+                base = base + jnp.where(counts, self.part(totals, i)[...], 0.0)
+            total = self.part(totals, x)[...]
+            before = jnp.zeros((self.size, HD), F32)
+            for i in range(NZ):
+                mine = self.part(pin, i)[...].astype(F32)
+                inside = jnp.where(self.ahead, before, total - before - mine)
+                self.part(pout, i)[...] = (base + inside).astype(BF16)
+                before = before + mine
+            entering[self.h, self.slice_of(z), :] = self.part(pout, z)[...]
+            for dz in far_first:
+                to = (z + dz) % NZ
+                self.send(2, self.part(pout, to), entering.at[self.h, self.slice_of(z), :], x * NZ + to)
+
+        def end(self):
+            self.landed(2, pout, NZ - 1, scan_recv)
+
+        def sent(self):
+            self.landed(0, pout, NZ - 1, scan_send)
+            self.landed(1, totals, NX - 1, scan_send)
+            self.landed(2, pout, NZ - 1, scan_send)
+
+    scan_0, scan_2, scan_3 = (Scan(n, n, 0, 2 * HD) for n in (0, 2, 3))
+    scan_1_keys, scan_1_queries = Scan(1, 1, 0, HD), Scan(4, 1, HD, HD)
+
+    head_0()
     block_states(0)
     later = NX - 1 - x + NZ - 1 - z
 
@@ -334,46 +417,67 @@
     def _():
         pl.semaphore_wait(up_sem, later)
 
-    scan_one(0)
+    scan_0.one()
+    head_1_keys()
+    block_states(1, (0,))
+    scan_1_keys.one()
     for n in (1, 2):
         pltpu.make_async_copy(early_in.at[n], early_in.at[n], early_recv.at[n]).wait()
-    for h in (2, 3):
+    for h, scan in ((2, scan_2), (3, scan_3)):
         block_states(h)
-        scan_one(h)
-    first_heads(1, 0, 3)
-    for h in (0, 2, 3):
-        scan_two(h)
-    first_heads(1, 3, 4)
-    block_states(1)
-    scan_one(1)
-    for h in (0, 2, 3):
-        scan_three(h)
+        scan.one()
+
+    def most(m, carry):
+        i = head_1_queries(m + m // 2)
+        near_parts(1, i, load(1, i))
+        return carry
+
+    lax.fori_loop(0, 3, most, 0)
+    first_scans = (scan_0, scan_1_keys, scan_2, scan_3)
+    for scan in first_scans:
+        scan.two()
+    last = head_1_queries(2)
+    block_states(1, (1,))
+    scan_1_queries.one()
+    for scan in first_scans:
+        scan.three()
+    near_parts(1, last, load(1, last))
     inner_states(0)
     inner_states(1)
-    scan_two(1)
-    scan_three(1)
-    scan_end(2)
-    last_heads(2)
-    whole(2, arrive(2, 2))
-    scan_end(3)
-    scan_end(0)
+    near(2, 0)
+    scan_1_queries.two()
+    near(2, 1)
+    near(2, 3)
+    other_states(2)
+    scan_1_queries.three()
+    near(2, 2)
+    scan_2.end()
+    finish(2)
+    scan_0.end()
     finish(0)
-    scan_end(1)
+    near(3, 0)
+    scan_3.end()
+    arrive(3, 1)
+    arrive(3, 3)
+    other_states(3)
+    far_parts(3, y)
+    for j in (1, 3):
+        i = (y + j) % NY
+        parts = load(3, i)
+        far = across(3, i, *parts)
+        store(3, i, [close + more for close, more in zip(within(*parts), far)])
+    scan_1_keys.end()
+    scan_1_queries.end()
     finish(1)
-    last_heads(3)
-    whole(3, arrive(3, 2))
+    whole(3, 2)
 
     sent = recv.at[:, :, pl.ds(0, 896), :]
     pltpu.make_async_copy(sent, sent, raw_send).wait()
     pltpu.make_async_copy(sib_out, sib_out, sib_send).wait()
     sent = early_in
     pltpu.make_async_copy(sent, sent, early_send).wait()
-    for n in range(4):
-        sent = pout.at[n, pl.ds(0, NZ - 1)]
-        pltpu.make_async_copy(sent, sent, scan_send.at[n, 0]).wait()
-        pltpu.make_async_copy(sent, sent, scan_send.at[n, 2]).wait()
-        sent = totals.at[n, pl.ds(0, NX - 1)]
-        pltpu.make_async_copy(sent, sent, scan_send.at[n, 1]).wait()
+    for scan in first_scans + (scan_1_queries,):
+        scan.sent()
 
 
 def write_out(a, b, c, d, out_a, out_b, out_c, out_d, sem):
@@ -397,7 +501,7 @@
         scratch_shapes=[
             pltpu.VMEM((4, 4, 1024, HD), BF16),
             pltpu.VMEM((4, 128, 4096), BF16),
-            pltpu.VMEM((4, 2, 1024, HD), F32),
+            pltpu.VMEM((4, 4, 1024, HD), F32),
             pltpu.VMEM((4, 4, HD, HD), F32),
             pltpu.VMEM((4, 4, HD, HD), F32),
             pltpu.VMEM((3, 4, HD, HD), BF16),
@@ -405,20 +509,21 @@
             pltpu.VMEM((4, HD, HD), F32),
             pltpu.VMEM((4, 4, 2, HD, HD), F32),
             pltpu.VMEM((4, 2 * HD, HD), BF16),
-            pltpu.VMEM((4, NZ, SLICE, HD), BF16),
-            pltpu.VMEM((4, NX, SLICE, HD), F32),
-            pltpu.VMEM((4, NZ, SLICE, HD), BF16),
+            pltpu.VMEM((5, NZ, SLICE, HD), BF16),
+            pltpu.VMEM((5, NX, SLICE, HD), F32),
+            pltpu.VMEM((5, NZ, SLICE, HD), BF16),
             pltpu.VMEM((4, 2 * HD, HD), BF16),
             pltpu.VMEM((4, 4, 2, HD, HD), BF16),
             dma,
-            dma((4, 4)),
+            dma((5, 4)),
             dma,
             dma,
             dma((4,)),
             dma,
             dma((3,)),
-            dma((4, 3)),
-            dma((4, 3)),
+            dma((5, 3)),
+            dma((5, 3)),
+            pltpu.SemaphoreType.REGULAR,
             pltpu.SemaphoreType.REGULAR,
         ],
         compiler_params=pltpu.CompilerParams(

time: 60.7 us -> 59.2 us (0.975)
  Pallas kernels: 59.9 us -> 57.9 us
    pallas_call x1, Pallas kernels: 57.9 us -> 55.8 us  [on_device(): pl.pallas_call(body, out_shape=[pltpu.VMEM((1024, 512), BF16)] * 4, in_sp...]
where the time goes in v3:
time: 59.2 us; the launch traced here: 58.5 us
  Pallas kernels  57.9 us (98%)
  between operations  0.64 us (1%)
    pallas_call x1, Pallas kernels, on_device(): pl.pallas_call(body, out_shape=[pltpu.VMEM((1024, 512), BF16)] * 4, in_sp...  55.8 us
    pallas_call x1, Pallas kernels, on_device(): pl.pallas_call(write_out, out_shape=[pltpu.HBM((1024, 512), BF16)] * 4, i...  2.02 us

profile of v3, /device:TPU:1, one launch (start us, length us, event | category | flops | bytes accessed | tf_op | source)
XLA Modules:
  0.0 58.5 jit_solution(12597328093811279281)
XLA Ops:
  0.6 55.8 %linear_attention.1 = (bf16[1024,512]{1,0:T(8,128)(2,1)S(1)}, bf16[1024,512]{1,0:T(8,128)(2,1)S(1)}, bf16[1024,512]{1,0:T(8,128)(2,1)S(1)}, bf16[1024,512]{1,0:T(8,128)(2,1)S(1)}) custom-call(bf16[128,4096]{1,0:T(8,128)(2,1)} %refs_0_.1, bf16[128,4096]{1,0:T(8,128)(2,1)} %refs_1_.1, bf16[128,4096]{1,0:T(8,128)(2,1)} %refs_2_.1, bf16[128,4096]{1,0:T(8,128)(2,1)} %refs_3_.1), custom_call_target="tpu_custom_call" | custom-call | tf_op jit(solution)/shard_map/linear_attention/pallas_call | solution.py:496
  56.5 2.0 %write_out.1 = (bf16[1024,512]{1,0:T(8,128)(2,1)}, bf16[1024,512]{1,0:T(8,128)(2,1)}, bf16[1024,512]{1,0:T(8,128)(2,1)}, bf16[1024,512]{1,0:T(8,128)(2,1)}) custom-call(bf16[1024,512]{1,0:T(8,128)(2,1)S(1)} %get-tuple-element.8.a, bf16[1024,512]{1,0:T(8,128)(2,1)S(1)} %get-tuple-element.9.b, bf16[1024,512]{1,0:T(8,128)(2,1)S(1)} %get-tuple-element.10.c, ...), custom_call_target="tpu_custom_call" | custom-call | tf_op jit(solution)/shard_map/write_out/pallas_call | solution.py:534

commit v4 on v3

--- a/solution.py
+++ b/solution.py
@@ -23,8 +23,23 @@
     )
 
 
+def within(qs, ks, vs, gs):
+    row = lax.broadcasted_iota(jnp.int32, (SUB, SUB), 0)
+    col = lax.broadcasted_iota(jnp.int32, (SUB, SUB), 1)
+    attn = jnp.where(row >= col, mm(qs, ks, 1, 1), 0.0).astype(BF16)
+    back = jnp.where(row >= col, mm(gs, vs, 1, 1), 0.0).astype(BF16)
+    return mm(attn, vs, 1, 0), mm(back, ks, 1, 0), mm(back, qs, 0, 0), mm(attn, gs, 0, 0)
+
+
+def with_states(parts, pre, suf, pre_in, suf_in):
+    qs, ks, vs, gs = (jnp.concatenate([rows, rows], axis=1) for rows in parts)
+    pre_rows, pre_cols = jnp.concatenate([pre, pre_in], axis=0), jnp.concatenate([pre, pre_in], axis=1)
+    suf_rows, suf_cols = jnp.concatenate([suf, suf_in], axis=0), jnp.concatenate([suf, suf_in], axis=1)
+    return mm(qs, pre_rows, 1, 0), mm(gs, pre_cols, 1, 1), mm(vs, suf_cols, 1, 1), mm(ks, suf_rows, 1, 0)
+
+
 def kernel(
-    scale, q, k, v, g, o0, o1, o2, o3,
+    scale, q, k, v, g, o0, o1, o2, o3, last_raw, last_states,
     recv, own, acc, sib_out, sib_in, early_out, early_in, onward, subs, states, pin, totals, pout,
     entering, inner, raw_send, raw_recv, own_sem, sib_send, sib_recv, early_send, early_recv,
     scan_send, scan_recv, up_sem, first_sem,
@@ -105,15 +120,18 @@
             for a in arrays:
                 raw(h, dy, dc, a).start()
 
-    def raw_to(h, ty, tc):
+    def raw_to(h, ty, tc, apart=False):
         to = ty * 2 + tc
 
         @pl.when(to != head)
         def _():
             for a in range(4):
+                rows = recv.at[a, h, pl.ds(pl.multiple_of(head * HD, HD), HD), :]
+                if apart:
+                    rows = last_raw.at[a, pl.ds(pl.multiple_of(core * HD, HD), HD), :]
                 pltpu.make_async_remote_copy(
                     src_ref=inputs[a].at[:, pl.ds(pl.multiple_of(to * 512 + h * HD, HD), HD)],
-                    dst_ref=recv.at[a, h, pl.ds(pl.multiple_of(head * HD, HD), HD), :],
+                    dst_ref=rows,
                     send_sem=raw_send,
                     recv_sem=raw_recv.at[h, (y + NY - ty) % NY],
                     device_id=(ctx, to),
@@ -123,7 +141,7 @@
     def send_last(h):
         for dy in (0, 1, 3, 2):
             for tc in (1, 0):
-                raw_to(h, (y + dy) % NY, tc)
+                raw_to(h, (y + dy) % NY, tc, dy == 2)
 
     keep(0, range(4))
     for dy, dc in peers:
@@ -204,33 +222,11 @@
     keep(3, range(4))
     send_last(3)
 
-    row = lax.broadcasted_iota(jnp.int32, (SUB, SUB), 0)
-    col = lax.broadcasted_iota(jnp.int32, (SUB, SUB), 1)
-    causal = row >= col
-
     def load(h, i):
         return tuple(recv[a, h, pl.ds(pl.multiple_of(i * SUB, SUB), SUB), :] for a in range(4))
 
-    def within(qs, ks, vs, gs):
-        attn = jnp.where(causal, mm(qs, ks, 1, 1), 0.0).astype(BF16)
-        back = jnp.where(causal, mm(gs, vs, 1, 1), 0.0).astype(BF16)
-        return mm(attn, vs, 1, 0), mm(back, ks, 1, 0), mm(back, qs, 0, 0), mm(attn, gs, 0, 0)
-
-    def across(h, i, qs, ks, vs, gs):
-        pre, suf = entering[h, 0:HD, :], entering[h, HD : 2 * HD, :]
-        pre_in, suf_in = inner[h, i, 0], inner[h, i, 1]
-
-        def twice(rows):
-            return jnp.concatenate([rows, rows], axis=1)
-
-        pre_rows, pre_cols = jnp.concatenate([pre, pre_in], axis=0), jnp.concatenate([pre, pre_in], axis=1)
-        suf_rows, suf_cols = jnp.concatenate([suf, suf_in], axis=0), jnp.concatenate([suf, suf_in], axis=1)
-        return (
-            mm(twice(qs), pre_rows, 1, 0),
-            mm(twice(gs), pre_cols, 1, 1),
-            mm(twice(vs), suf_cols, 1, 1),
-            mm(twice(ks), suf_rows, 1, 0),
-        )
+    def across(h, i, parts):
+        return with_states(parts, entering[h, 0:HD, :], entering[h, HD : 2 * HD, :], inner[h, i, 0], inner[h, i, 1])
 
     def arrive(h, j):
         i = (y + j) % NY
@@ -283,13 +279,7 @@
 
     def whole(h, i):
         parts = load(h, i)
-        far = across(h, i, *parts)
-        store(h, i, [close + more for close, more in zip(within(*parts), far)])
-
-    def whole(h, j):
-        i = arrive(h, j)
-        parts = load(h, i)
-        far = across(h, i, *parts)
+        far = across(h, i, parts)
         store(h, i, [close + more for close, more in zip(within(*parts), far)])
 
     def near(h, j):
@@ -308,7 +298,7 @@
 
     def far_parts(h, i):
         rows = pl.ds(pl.multiple_of(i * SUB, SUB), SUB)
-        far = across(h, i, *load(h, i))
+        far = across(h, i, load(h, i))
         store(h, i, [acc[n, h, rows, :] + more for n, more in enumerate(far)])
 
     def finish(h):
@@ -461,15 +451,18 @@
     arrive(3, 3)
     other_states(3)
     far_parts(3, y)
+    for st in range(2):
+        last_states[st] = entering[3, pl.ds(st * HD, HD), :]
+        last_states[2 + st] = inner[3, (y + 2) % NY, st]
     for j in (1, 3):
         i = (y + j) % NY
         parts = load(3, i)
-        far = across(3, i, *parts)
+        far = across(3, i, parts)
         store(3, i, [close + more for close, more in zip(within(*parts), far)])
     scan_1_keys.end()
     scan_1_queries.end()
     finish(1)
-    whole(3, 2)
+    pltpu.make_async_copy(last_raw, last_raw, raw_recv.at[3, 2]).wait()
 
     sent = recv.at[:, :, pl.ds(0, 896), :]
     pltpu.make_async_copy(sent, sent, raw_send).wait()
@@ -480,24 +473,50 @@
         scan.sent()
 
 
-def write_out(a, b, c, d, out_a, out_b, out_c, out_d, sem):
-    pairs = ((a, out_a), (b, out_b), (c, out_c), (d, out_d))
-    for src, dst in pairs:
-        pltpu.make_async_copy(src, dst, sem).start()
-    for src, dst in pairs:
-        pltpu.make_async_copy(src, dst, sem).wait()
+def write_out(
+    scale, a, b, c, d, last_raw, last_states, out_a, out_b, out_c, out_d, last, sem, last_sem
+):
+    place = (lax.axis_index("head") // 2 + 2) % NY
+
+    def rows_of(i):
+        return pl.ds(pl.multiple_of(i * SUB, SUB), SUB)
+
+    most, rest = pl.ds(0, 3 * HD), pl.ds(3 * HD, HD)
+    copies = []
+    for src, dst in ((a, out_a), (b, out_b), (c, out_c), (d, out_d)):
+        for n in range(1, NY):
+            rows = rows_of((place + n) % NY)
+            copies.append(pltpu.make_async_copy(src.at[rows, :], dst.at[rows, :], sem))
+        rows = rows_of(place)
+        copies.append(pltpu.make_async_copy(src.at[rows, most], dst.at[rows, most], sem))
+    for copy in copies:
+        copy.start()
+    parts = tuple(last_raw[n] for n in range(4))
+    far = with_states(parts, *(last_states[n] for n in range(4)))
+    for n, (close, more, dst) in enumerate(zip(within(*parts), far, (out_a, out_b, out_c, out_d))):
+        last[n] = ((close + more) * scale).astype(BF16)
+        copies.append(pltpu.make_async_copy(last.at[n], dst.at[rows_of(place), rest], last_sem))
+        copies[-1].start()
+    for copy in copies:
+        copy.wait()
 
 
 def on_device(queries, key_rows, value_rows, out_grad):
+    scale = 1.0 / math.sqrt(4194304)
+
     def body(*refs):
-        kernel(1.0 / math.sqrt(4194304), *refs)
+        kernel(scale, *refs)
+
+    def write_body(*refs):
+        write_out(scale, *refs)
 
     dma = pltpu.SemaphoreType.DMA
     results = pl.pallas_call(
         body,
-        out_shape=[pltpu.VMEM((1024, 512), BF16)] * 4,
+        out_shape=[pltpu.VMEM((1024, 512), BF16)] * 4
+        + [pltpu.VMEM((4, SUB, HD), BF16), pltpu.VMEM((4, HD, HD), BF16)],
         in_specs=[pl.BlockSpec(memory_space=pl.ANY)] * 4,
-        out_specs=[pl.BlockSpec(memory_space=pltpu.VMEM)] * 4,
+        out_specs=[pl.BlockSpec(memory_space=pltpu.VMEM)] * 6,
         scratch_shapes=[
             pltpu.VMEM((4, 4, 1024, HD), BF16),
             pltpu.VMEM((4, 128, 4096), BF16),
@@ -532,11 +551,11 @@
         name="linear_attention",
     )(queries, key_rows, value_rows, out_grad)
     return pl.pallas_call(
-        write_out,
+        write_body,
         out_shape=[pltpu.HBM((1024, 512), BF16)] * 4,
-        in_specs=[pl.BlockSpec(memory_space=pltpu.VMEM)] * 4,
+        in_specs=[pl.BlockSpec(memory_space=pltpu.VMEM)] * 6,
         out_specs=[pl.BlockSpec(memory_space=pltpu.HBM)] * 4,
-        scratch_shapes=[dma],
+        scratch_shapes=[pltpu.VMEM((4, SUB, HD), BF16), dma, dma],
         compiler_params=pltpu.CompilerParams(vmem_limit_bytes=VMEM_LIMIT),
         name="write_out",
     )(*[pltpu.with_memory_space_constraint(result, pltpu.VMEM) for result in results])

time: 59.2 us -> 58.6 us (0.990)
  Pallas kernels: 57.9 us -> 57.2 us
    pallas_call x2, Pallas kernels: 57.9 us -> 57.2 us  [the longest x1 55.2 us: on_device(): pl.pallas_call(body, out_shape=[pltpu.VMEM((1024, 512), BF16)] * 4 + [plt...]
where the time goes in v4:
time: 58.6 us; the launch traced here: 57.9 us
  Pallas kernels  57.2 us (98%)
  between operations  0.64 us (1%)
    pallas_call x1, Pallas kernels, on_device(): pl.pallas_call(body, out_shape=[pltpu.VMEM((1024, 512), BF16)] * 4 + [plt...  55.2 us
    pallas_call x1, Pallas kernels, on_device(): pl.pallas_call(write_body, out_shape=[pltpu.HBM((1024, 512), BF16)] * 4,...  2.02 us

profile of v4, /device:TPU:1, one launch (start us, length us, event | category | flops | bytes accessed | tf_op | source)
XLA Modules:
  0.0 57.9 jit_solution(15452950306940596911)
XLA Ops:
  0.6 55.2 %linear_attention.1 = (bf16[1024,512]{1,0:T(8,128)(2,1)S(1)}, bf16[1024,512]{1,0:T(8,128)(2,1)S(1)}, bf16[1024,512]{1,0:T(8,128)(2,1)S(1)}, bf16[1024,512]{1,0:T...) custom-call(bf16[128,4096]{1,0:T(8,128)(2,1)} %refs_0_.1, ...), custom_call_target="tpu_custom_call" | custom-call | tf_op jit(solution)/shard_map/linear_attention/pallas_call | solution.py:514
  55.9 2.0 %write_out.1 = (bf16[1024,512]{1,0:T(8,128)(2,1)}, bf16[1024,512]{1,0:T(8,128)(2,1)}, bf16[1024,512]{1,0:T(8,128)(2,1)}, bf16[1024,512]{1,0:T(8,128)(2,1)}) custom-call(bf16[1024,512]{1,0:T(8,128)(2,1)S(1)} %get-tuple-element.10.refs_0_, bf16[1024,512]{1,0:T(8,128)(2,1)S(1)} %get-tuple-element.11.refs_1_, bf16[1024,512]{1,0:T(8,128)(2,1)S(1)} %get-tuple-element.12.refs_2_, ...), custom_call_target="tpu_custom_call" | custom-call | tf_op jit(solution)/shard_map/write_out/pallas_call | solution.py:553
